TPU v7x, 32 devices: a whole 2x2x4 slice. The times are simulated.
32 devices in a mesh: groups: 2 (over y), block: 4 (over z), scen: 2 (over x), dp: 2 (over core).
Axes of the slice: x: 2, y: 2, z: 4, core: 2. Of those that a mesh axis runs over, the one named last changes fastest.
Arguments:
- grad_parts: bfloat16 [2, 4, 8, 512, 512], P('dp', ('groups', 'scen'), None, 'block'), parts along dimension 1, may hold values from -16 to 16
- live_counts: int32 [4], P('groups'), parts along dimension 0, may hold values from 1 to 6, as said below
Outputs:
- direction: bfloat16 [4, 8, 512, 512], P(('groups', 'scen'), None, ('block', 'dp')), parts along dimension 0
There are 2 independent parts, one for each index of `groups`. A program takes and returns all parts, laid end to end along the dimension named above; each array names one. Nothing has to cross between parts.
Inputs may be any that keep to these rules, and one draw needn't show every extreme that they name: `live_counts`: exactly one tower has 6 live slots; every other tower has at most 2, so the counts of all towers sum to at most 8.
All inputs are finite; a program needn't handle non-finite values.
Results may differ from a plain program's by a relative error of at most 0.001.
The roundings to bfloat16 on the way count: a program that leaves them out, or rounds other values in their place, can miss the bound.
Values may be sent and summed in bfloat16 or wider, within the bound.
A program may use at most 64 MiB of HBM per device.

v0:
```python
import jax
import jax.numpy as jnp
from jax import lax
from jax.sharding import PartitionSpec as P

ITERS = 2


DAMPING = 0.25
EPSILON = 1e-06
HIGHEST = lax.Precision.HIGHEST


def for_sending(shard):

    def short(part):
        return part.astype(jnp.bfloat16) if part.dtype == jnp.float32 else part

    return jax.tree.map(short, shard)


def swapped(value, axis, apart):
    mask = 2**apart
    pairs = [(source, source ^ mask) for source in range(lax.axis_size(axis))]
    return lax.ppermute(value, axis, pairs)


def newton_root(statistics):
    extent = statistics.shape[0]
    identity = jnp.eye(extent, dtype=jnp.float32)
    damped = statistics + (DAMPING * jnp.trace(statistics) / extent + EPSILON) * identity
    scaled = damped / (2.0 * jnp.trace(damped) / extent)
    inverse = identity
    for iteration in range(ITERS):
        factor = (5.0 * identity - scaled) * 0.25
        if iteration == 0:
            inverse = factor
        else:
            inverse = jnp.dot(
                inverse, factor, precision=HIGHEST, preferred_element_type=jnp.float32
            )
        if iteration + 1 < ITERS:
            square = jnp.dot(factor, factor, precision=HIGHEST, preferred_element_type=jnp.float32)
            fourth = jnp.dot(square, square, precision=HIGHEST, preferred_element_type=jnp.float32)
            scaled = jnp.dot(fourth, scaled, precision=HIGHEST, preferred_element_type=jnp.float32)
    return inverse.astype(jnp.bfloat16)


def owner_roots(blocks, live_flags, pair_index):

    def single(element):
        gradient, live_flag = element
        operand = jnp.where(pair_index == 0, gradient, gradient.T)

        def compute(unused):
            statistics = jnp.dot(operand, operand.T, preferred_element_type=jnp.float32)
            return newton_root(statistics)

        def skipped(unused):
            return jnp.zeros(gradient.shape, jnp.bfloat16)

        return lax.cond(live_flag > 0, compute, skipped, 0)

    return lax.map(single, (blocks, live_flags))


def directions(blocks, live_flags, pair_index, owners_count):
    own_roots = owner_roots(blocks, live_flags, pair_index)
    others = jax.tree.map(
        lambda part, own: part.astype(own.dtype),
        swapped(for_sending(own_roots), "dp", 0),
        own_roots,
    )
    left_roots = jnp.where(pair_index == 0, own_roots, others)
    right_roots = jnp.where(pair_index == 0, others, own_roots)
    slot_count = blocks.shape[0]
    extent = blocks.shape[1]
    halves = extent // (2 * owners_count)
    split_rows = left_roots.reshape(slot_count, owners_count, 2, halves, extent)
    chosen = lax.dynamic_index_in_dim(split_rows, pair_index, 2, keepdims=False)
    chosen = chosen.reshape(slot_count, owners_count * halves, extent)
    inner_rows = jnp.einsum(
        "srk,skc->src", chosen, blocks, preferred_element_type=jnp.float32
    ).astype(jnp.bfloat16)
    raw_direction = jnp.einsum(
        "src,scd->srd", inner_rows, right_roots, preferred_element_type=jnp.float32
    )
    grad_square = jnp.sum(jnp.square(blocks.astype(jnp.float32)), axis=(1, 2))
    part_square = jnp.sum(raw_direction * raw_direction, axis=(1, 2))
    total_square = lax.psum(part_square, "dp")
    entries = float(extent * extent)
    graft_scale = (
        live_flags * jnp.sqrt(grad_square / entries) / jnp.sqrt(total_square / entries + EPSILON)
    )
    return (raw_direction * graft_scale[:, None, None]).astype(jnp.bfloat16)


def shards(grad_parts, live_counts):
    grad_shard = grad_parts[0, 0]
    owners_count = lax.axis_size("block")
    pair_index = lax.axis_index("dp")
    tower_index = lax.axis_index("scen")
    place_index = lax.axis_index("block")
    slot_total, shard_rows, extent = grad_shard.shape
    per_owner = slot_total // owners_count
    half_rows = shard_rows // 2
    own_live = live_counts[tower_index]
    partial_value = grad_shard.astype(jnp.float32)
    summed = lax.psum(partial_value.astype(jnp.bfloat16), "dp")
    sent_rows = summed.shape[1]
    outgoing = summed.reshape(per_owner, owners_count, sent_rows, extent)
    received = lax.all_to_all(outgoing, "block", split_axis=1, concat_axis=1, tiled=True)
    blocks = received.reshape(received.shape[0], extent, extent)
    slot_ids = jnp.arange(per_owner, dtype=jnp.int32) * owners_count + place_index
    live_flags = (slot_ids < own_live).astype(jnp.float32)
    result = directions(blocks, live_flags, pair_index, owners_count)
    returning = result.reshape(per_owner, owners_count, half_rows, extent)
    arrived = lax.all_to_all(returning, "block", split_axis=1, concat_axis=1, tiled=True)
    own_rows = arrived.reshape(slot_total, half_rows, extent)
    return own_rows[None]


def solution(mesh):
    in_specs = (P("dp", ("groups", "scen"), None, "block", None), P("groups"))
    out_specs = P(("groups", "scen"), None, ("block", "dp"), None)
    return jax.shard_map(shards, mesh=mesh, in_specs=in_specs, out_specs=out_specs, check_vma=False)
```

profile of v0, /device:TPU:0, one launch (start us, length us, event | category | flops | bytes accessed | tf_op | source)
XLA Modules:
  0.0 131.1 jit_solution(4809111121688937410)
XLA Ops:
  6.5 0.0 all-reduce.2.cloned.1.call-start
  6.5 0.7 all-reduce.2.cloned.1.call-update
  7.3 24.8 %all-reduce.2.cloned.1.call-done = bf16[2,4,128,512]{3,2,1,0:T(8,128)(2,1)} async-done(((bf16[2,4,128,512]{3,2,1,0:T(8,128)(2,1)}), bf16[2,4,128,512]{3,2,1,0:T(8,128)(2,1)}) %all-reduce.2.cloned.1.call-update) | async-done | bytes 1048592 | tf_op jit(solution)/shard_map/psum | solution.py:109
  32.0 2.3 %copy.7 = bf16[2,4,128,512]{3,2,0,1:T(8,128)(2,1)} copy(bf16[2,4,128,512]{3,2,1,0:T(8,128)(2,1)} %all-reduce.2.cloned.1.call-done) | data formatting | bytes 2097152 | tf_op jit(solution)/shard_map/psum | solution.py:109
  34.3 0.0 copy-start.1
  34.3 5.0 %all-to-all-start = ((bf16[2,4,128,512]{3,2,0,1:T(8,128)(2,1)}), bf16[2,4,128,512]{3,2,0,1:T(8,128)(2,1)S(1)}, u32[]{:S(2)}, u32[]{:S(2)}) async-start(bf16[2,4,128,512]{3,2,0,1:T(8,128)(2,1)} %copy.7), calls=%async_computation | async-start | bytes 2097152 | tf_op jit(solution)/shard_map/all_to_all | solution.py:112
  39.3 0.0 copy-done.1
  39.3 0.6 dynamic_slice.19
  39.9 0.6 compare_convert_fusion
  40.5 25.0 %all-to-all-done = bf16[2,4,128,512]{3,2,0,1:T(8,128)(2,1)S(1)} async-done(((bf16[2,4,128,512]{3,2,0,1:T(8,128)(2,1)}), bf16[2,4,128,512]{3,2,0,1:T(8,128)(2,1)S(1)}, u32[]{:S(2)}, u32[]{:S(2)}) %all-to-all-start) | async-done | bytes 1048608 | tf_op jit(solution)/shard_map/all_to_all | solution.py:112
  65.5 1.1 copy.8
  66.5 27.9 %while.12 = (s32[]{:T(128)}, bf16[2,512,512]{2,1,0:T(8,128)(2,1)}, f32[2]{0:T(128)S(1)}, bf16[2,512,512]{2,1,0:T(8,128)(2,1)}, pred[]{:T(512)}, /*index=5*/s32[]{:T(128)}, f32[1]{0:T(128)}) while((s32[]{:T(128)}, bf16[2,512,512]{2,1,0:T(8,128)(2,1)}, f32[2]{0:T(128)S(1)}, bf16[2,512,512]{2,1,0:T(8,128)(2,1)}, pred[]{:T(512)}, ...), condition=%wide.region_6.7_spmd, body=%wide.region_1.6_spmd.sunk | while | flops 6719275008 | bytes 16253152 | solution.py:64
  66.5 0.6 dynamic_slice.26
  67.8 1.1 dynamic-slice_bitcast_fusion.2
  68.8 0.2 copy.14
  69.1 10.6 %conditional.2 = (bf16[1,512,512]{2,1,0:T(8,128)(2,1)S(1)}) conditional(s32[]{:T(128)} %bitcast.25, () %tuple.40, (pred[]{:T(512)}, bf16[512,512]{1,0:T(8,128)(2,1)S(1)}, bf16[512,512]{1,0:T(8,128)(2,1)S(1)}) %tuple.49), branch_computations={%region_2.2_spmd, %region_3.5_spmd} | conditional | flops 6719275008 | bytes 13107281 | solution.py:62
  69.1 1.0 select_reduce_fusion.1
  70.7 0.6 select_reduce_fusion
  71.9 2.0 %fusion.5 = f32[512,512]{1,0:T(8,128)S(1)} fusion(f32[512,512]{1,0:T(8,128)S(1)} %get-tuple-element.95, f32[]{:T(128)S(6)} %div.15, f32[]{:T(128)S(6)} %add.23), kind=kOutput, calls=%fused_computation.11 | convolution fusion | flops 1612447744 | bytes 2097160 | tf_op jit(solution)/shard_map/while/body/eval_jaxpr/cond/branch_1_fun/dot_general | solution.py:43
  73.9 1.8 %fusion.29 = f32[512,512]{1,0:T(8,128)S(1)} fusion(f32[512,512]{1,0:T(8,128)S(1)} %fusion.5), kind=kOutput, calls=%fused_computation.42 | convolution fusion | flops 1610612736 | bytes 2097152 | tf_op jit(solution)/shard_map/while/body/eval_jaxpr/cond/branch_1_fun/dot_general | solution.py:44
  75.7 1.9 %fusion = f32[512,512]{1,0:T(8,128)S(1)} fusion(f32[512,512]{1,0:T(8,128)S(1)} %fusion.29, f32[512,512]{1,0:T(8,128)S(1)} %get-tuple-element.95, f32[]{:T(128)S(6)} %div.15, f32[]{:T(128)S(6)} %add.23), kind=kOutput, calls=%fused_computation.2 | convolution fusion | flops 1612709888 | bytes 3145736 | tf_op jit(solution)/shard_map/while/body/eval_jaxpr/cond/branch_1_fun/dot_general | solution.py:45
  77.6 2.0 %fusion.1 = bf16[1,512,512]{2,1,0:T(8,128)(2,1)S(1)} fusion(f32[512,512]{1,0:T(8,128)S(1)} %fusion, f32[512,512]{1,0:T(8,128)S(1)} %get-tuple-element.95, f32[]{:T(128)S(6)} %div.15, f32[]{:T(128)S(6)} %add.23), kind=kOutput, calls=%fused_computation.4 | convolution fusion | flops 1612709888 | bytes 2621448 | tf_op jit(solution)/shard_map/while/body/eval_jaxpr/cond/branch_1_fun/dot_general | solution.py:39
  79.6 0.9 constant_dynamic-update-slice_fusion.2
  80.5 0.6 dynamic_slice.26
  81.7 1.1 dynamic-slice_bitcast_fusion.2
  82.8 0.2 copy.14
  83.0 10.6 %conditional.2 = (bf16[1,512,512]{2,1,0:T(8,128)(2,1)S(1)}) conditional(s32[]{:T(128)} %bitcast.25, () %tuple.40, (pred[]{:T(512)}, bf16[512,512]{1,0:T(8,128)(2,1)S(1)}, bf16[512,512]{1,0:T(8,128)(2,1)S(1)}) %tuple.49), branch_computations={%region_2.2_spmd, %region_3.5_spmd} | conditional | flops 6719275008 | bytes 13107281 | solution.py:62
  83.0 1.1 select_reduce_fusion.1
  84.6 0.6 select_reduce_fusion
  85.8 2.0 %fusion.5 = f32[512,512]{1,0:T(8,128)S(1)} fusion(f32[512,512]{1,0:T(8,128)S(1)} %get-tuple-element.95, f32[]{:T(128)S(6)} %div.15, f32[]{:T(128)S(6)} %add.23), kind=kOutput, calls=%fused_computation.11 | convolution fusion | flops 1612447744 | bytes 2097160 | tf_op jit(solution)/shard_map/while/body/eval_jaxpr/cond/branch_1_fun/dot_general | solution.py:43
  87.8 1.8 %fusion.29 = f32[512,512]{1,0:T(8,128)S(1)} fusion(f32[512,512]{1,0:T(8,128)S(1)} %fusion.5), kind=kOutput, calls=%fused_computation.42 | convolution fusion | flops 1610612736 | bytes 2097152 | tf_op jit(solution)/shard_map/while/body/eval_jaxpr/cond/branch_1_fun/dot_general | solution.py:44
  89.7 1.9 %fusion = f32[512,512]{1,0:T(8,128)S(1)} fusion(f32[512,512]{1,0:T(8,128)S(1)} %fusion.29, f32[512,512]{1,0:T(8,128)S(1)} %get-tuple-element.95, f32[]{:T(128)S(6)} %div.15, f32[]{:T(128)S(6)} %add.23), kind=kOutput, calls=%fused_computation.2 | convolution fusion | flops 1612709888 | bytes 3145736 | tf_op jit(solution)/shard_map/while/body/eval_jaxpr/cond/branch_1_fun/dot_general | solution.py:45
  91.6 2.0 %fusion.1 = bf16[1,512,512]{2,1,0:T(8,128)(2,1)S(1)} fusion(f32[512,512]{1,0:T(8,128)S(1)} %fusion, f32[512,512]{1,0:T(8,128)S(1)} %get-tuple-element.95, f32[]{:T(128)S(6)} %div.15, f32[]{:T(128)S(6)} %add.23), kind=kOutput, calls=%fused_computation.4 | convolution fusion | flops 1612709888 | bytes 2621448 | tf_op jit(solution)/shard_map/while/body/eval_jaxpr/cond/branch_1_fun/dot_general | solution.py:39
  93.6 0.9 constant_dynamic-update-slice_fusion.2
  94.4 0.0 copy-start
  94.4 0.0 collective-permute-start
  94.4 0.4 multiply_reduce_fusion
  94.8 2.5 %collective-permute-done = bf16[2,512,512]{2,1,0:T(8,128)(2,1)S(1)} collective-permute-done((bf16[2,512,512]{2,1,0:T(8,128)(2,1)}, bf16[2,512,512]{2,1,0:T(8,128)(2,1)S(1)}, u32[]{:S(2)}, u32[]{:S(2)}) %collective-permute-start) | collective-permute-done | bytes 1048608 | tf_op jit(solution)/shard_map/ppermute | solution.py:25
  97.3 0.0 copy-done
  97.3 0.1 broadcast_select_fusion
  97.4 0.8 constant_dynamic-slice_fusion
  98.3 3.1 %multiply_reduce_fusion.1 = (f32[2]{0:T(128)S(1)}, f32[2,256,512]{2,1,0:T(8,128)}) fusion(bf16[2,512,512]{2,1,0:T(8,128)(2,1)S(1)} %collective-permute-done, bf16[2,512,512]{2,1,0:T(8,128)(2,1)S(1)} %copy-done, pred[]{:T(512)} %eq.21, bf16[2,256,512]{2,1,0:T(8,128)(2,1)} %bitcast.31, bf16[2,512,512]{2,1,0:T(8,128)(2,1)} %bitcast.6), kind=kOutput, calls=%fused_computation.33 | convolution fusion | flops 538181632 | bytes 4718601 | tf_op jit(solution)/shard_map/src,scd->srd/dot_general | solution.py:85
  101.4 2.4 %psum.15 = f32[2]{0:T(128)S(1)} all-reduce(f32[2]{0:T(128)S(1)} %get-tuple-element.96), channel_id=1, replica_groups=mesh['groups'=2,'block'=4,'scen'=2,'dp'=2] {'dp'}, use_global_device_ids=true, to_apply=%region_9.10 | all-reduce | flops 2 | bytes 16 | tf_op jit(solution)/shard_map/psum | solution.py:90
  103.8 0.6 fusion.28
  104.5 1.4 %multiply_convert_fusion = bf16[2,256,512]{2,1,0:T(8,128)(2,1)S(1)} fusion(f32[2,256,512]{2,1,0:T(8,128)} %get-tuple-element.97, f32[2]{0:T(128)S(1)} %fusion.28), kind=kLoop, calls=%fused_computation.32 | loop fusion | flops 524288 | bytes 1572872 | tf_op jit(solution)/shard_map/convert_element_type | solution.py:95
  105.9 17.5 %all_to_all.10 = bf16[2,4,64,512]{3,2,0,1:T(8,128)(2,1)S(1)} all-to-all(bf16[2,4,64,512]{3,2,0,1:T(8,128)(2,1)S(1)} %copy.10), channel_id=1, replica_groups=mesh['groups'=2,'block'=4,'scen'=2,'dp'=2] {'block'}, dimensions={1} | all-to-all | bytes 1048576 | tf_op jit(solution)/shard_map/all_to_all | solution.py:118
  123.4 0.8 copy.11
  (2 shorter events, 0.0 us)
Async XLA Ops:
  6.5 25.5 %all-reduce.2.cloned.1.call-start = ((), (), s32[]{:S(2)}) async-start(), calls=%async_computation.2 | async-start | bytes 2097152 | tf_op jit(solution)/shard_map/psum | solution.py:109
  34.3 5.0 %copy-start.1 = (s32[2]{0:T(128)S(1)}, s32[2]{0:T(128)}, u32[]{:S(2)}) copy-start(s32[2]{0:T(128)} %param.7) | copy-start | bytes 28
  34.3 31.2 %all-to-all-start = ((bf16[2,4,128,512]{3,2,0,1:T(8,128)(2,1)}), bf16[2,4,128,512]{3,2,0,1:T(8,128)(2,1)S(1)}, u32[]{:S(2)}, u32[]{:S(2)}) async-start(bf16[2,4,128,512]{3,2,0,1:T(8,128)(2,1)} %copy.7), calls=%async_computation | async-start | bytes 2097152 | tf_op jit(solution)/shard_map/all_to_all | solution.py:112
  94.4 2.9 %copy-start = (bf16[2,512,512]{2,1,0:T(8,128)(2,1)S(1)}, bf16[2,512,512]{2,1,0:T(8,128)(2,1)}, u32[]{:S(2)}) copy-start(bf16[2,512,512]{2,1,0:T(8,128)(2,1)} %get-tuple-element.83) | copy-start | bytes 3145732
  94.4 2.9 %collective-permute-start = (bf16[2,512,512]{2,1,0:T(8,128)(2,1)}, bf16[2,512,512]{2,1,0:T(8,128)(2,1)S(1)}, u32[]{:S(2)}, u32[]{:S(2)}) collective-permute-start(bf16[2,512,512]{2,1,0:T(8,128)(2,1)} %get-tuple-element.83), channel_id=1, source_target_pairs={{0,1},{1,0},{2,3},{3,2},{4,5},{5,4},{6,7},{7,6},{8,9},{9,8},{10,11... | collective-permute-start | bytes 3145736 | tf_op jit(solution)/shard_map/ppermute | solution.py:25
Sparse Core Ops, SparseCore 0:
  9.7 22.2 all-reduce.1
where the time goes:
time: 132 us; the launch traced here: 131 us
  waiting for transfers between devices  52.9 us (40%)
  matrix products  20.7 us (16%)
  blocking collectives  19.9 us (15%)
  between operations  13.4 us (10%)
  local copies, waits for them, and re-layouts  11.1 us (8%)
  starting transfers between devices  5.01 us (4%)
  other arithmetic  4.41 us (3%)
  loops' own time  3.59 us (3%)
    all_to_all x1, waiting for transfers between devices, shards(): lax.all_to_all(outgoing, 'block', split_axis=1, concat_axis=1, tiled=True)  25 us
    psum x1, waiting for transfers between devices, shards(): summed = lax.psum(partial_value.astype(jnp.bfloat16), 'dp')  24.8 us
    all_to_all x1, blocking collectives, shards(): lax.all_to_all(returning, 'block', split_axis=1, concat_axis=1, tiled=True)  17.5 us
    all_to_all x1, starting transfers between devices, shards(): lax.all_to_all(outgoing, 'block', split_axis=1, concat_axis=1, tiled=True)  5 us
    dot_general x2, matrix products, newton_root(): jnp.dot(factor, factor, precision=HIGHEST, preferred_element_type=jnp.flo...  4 us
    dot_general x2, matrix products, newton_root(): jnp.dot(inverse, factor, precision=HIGHEST, preferred_element_type=jnp.fl...  3.95 us
    dot_general x2, matrix products, newton_root(): jnp.dot(fourth, scaled, precision=HIGHEST, preferred_element_type=jnp.flo...  3.8 us
    dot_general x2, matrix products, newton_root(): jnp.dot(square, square, precision=HIGHEST, preferred_element_type=jnp.flo...  3.68 us
  transfers between devices with their start and end apart: 3, of which 3 were waited for; matrix products, arithmetic and copies ran while one was open for 1% of the time, Pallas kernels for 0%

commit v1 on v0

v1 whole, which is shorter than its diff:
```python
import functools

import jax
import jax.numpy as jnp
from jax import lax
from jax.experimental import pallas as pl
from jax.experimental.pallas import tpu as pltpu
from jax.sharding import PartitionSpec as P

DAMPING = 0.25
EPSILON = 1e-06
MESH = pl.DeviceIdType.MESH
F32 = jnp.float32
BF16 = jnp.bfloat16
MEAN = 1.125
STRIPES = 4


def product(a, b, contract=((1,), (0,))):
    return lax.dot_general(a, b, (contract, ((), ())), preferred_element_type=F32)


def split(value):
    high = value.astype(BF16)
    return high, (value - high.astype(F32)).astype(BF16)


def refresh(
    counts, grad, ret, xret,
    own, peer, summed, arrived, chosen, gbuf, work, half, high1, low1, high2, low2,
    inner, rroot, outgoing,
    own_sem, pair_send, pair_recv, x_send, x_recv, z_send, z_recv, f_send, f_recv,
    r_send, r_recv, o_send, o_recv, y_send, y_recv, local_sem,
):
    owners = lax.axis_size("block")
    extra = owners // 2
    extent = gbuf.shape[0]
    rows = extent // owners
    part = rows // 2
    core = lax.axis_index("dp")
    place = lax.axis_index("block")
    tower = lax.axis_index("scen")
    other_tower = tower + 1 - 2 * lax.rem(tower, 2)
    sibling = {"dp": 1 - core}
    across = {"scen": other_tower}

    def aligned(index):
        return pl.multiple_of(index, part)

    groups = ((owners, extra), (0, extra), (extra, owners - extra))

    def own_copy(i):
        first, count = groups[i]
        return pltpu.make_async_copy(
            grad.at[pl.ds(first, count), pl.ds(aligned(core * part), part), :],
            own.at[pl.ds(first, count)],
            own_sem.at[i],
        )

    def pair_copy(i):
        first, count = groups[i]
        return pltpu.make_async_remote_copy(
            src_ref=grad.at[pl.ds(first, count), pl.ds(aligned((1 - core) * part), part), :],
            dst_ref=peer.at[pl.ds(first, count)],
            send_sem=pair_send.at[i],
            recv_sem=pair_recv.at[i],
            device_id=sibling,
            device_id_type=MESH,
        )

    def x_copy(k):
        return pltpu.make_async_remote_copy(
            src_ref=summed.at[owners + k],
            dst_ref=arrived.at[k],
            send_sem=x_send.at[k],
            recv_sem=x_recv.at[k],
            device_id=across,
            device_id_type=MESH,
        )

    def own_rows(index):
        return pl.ds(aligned(index * rows + core * part), part)

    def z_copy(owner, source, source_place):
        return pltpu.make_async_remote_copy(
            src_ref=source,
            dst_ref=gbuf.at[own_rows(source_place)],
            send_sem=z_send.at[owner],
            recv_sem=z_recv.at[source_place],
            device_id={"block": owner},
            device_id_type=MESH,
        )

    def f_copy(index):
        return pltpu.make_async_remote_copy(
            src_ref=gbuf.at[own_rows(index)],
            dst_ref=gbuf.at[own_rows(index)],
            send_sem=f_send.at[index],
            recv_sem=f_recv.at[index],
            device_id=sibling,
            device_id_type=MESH,
        )

    for i in range(3):
        own_copy(i).start()

    barrier = pltpu.get_barrier_semaphore()
    pl.semaphore_signal(barrier, inc=1, device_id=sibling, device_id_type=MESH)
    pl.semaphore_signal(barrier, inc=1, device_id=across, device_id_type=MESH)
    for step in range(1, owners):
        pl.semaphore_signal(
            barrier,
            inc=1,
            device_id={"block": lax.rem(place + step, owners)},
            device_id_type=MESH,
        )
    pl.semaphore_wait(barrier, owners + 1)

    for i in range(3):
        pair_copy(i).start()

    def add_pair(i):
        first, count = groups[i]
        own_copy(i).wait()
        pair_copy(i).wait_recv()
        for slot in range(first, first + count):
            summed[slot] = (own[slot].astype(F32) + peer[slot].astype(F32)).astype(BF16)

    def give(owner, source):
        @pl.when(place != owner)
        def _():
            z_copy(owner, source, place).start()

        @pl.when(place == owner)
        def _():
            gbuf[own_rows(owner), :] = source[...]
            f_copy(owner).start()

    add_pair(0)
    for k in range(extra):
        x_copy(k).start()
    add_pair(1)
    for k in range(extra):
        give(2 * k, summed.at[k])
    add_pair(2)
    own_live = counts[tower]
    other_live = counts[other_tower]
    fullest = own_live > extra
    is_fullest = jnp.broadcast_to(own_live, (part, extent)) > extra
    for k in range(extra):
        x_copy(k).wait_recv()
        chosen[k] = jnp.where(
            is_fullest, summed[extra + k].astype(F32), arrived[k].astype(F32)
        ).astype(BF16)
        give(2 * k + 1, chosen.at[k])

    for step in range(1, owners):
        source = lax.rem(place + step, owners)
        z_copy(place, chosen.at[0], source).wait_recv()
        f_copy(source).start()
    for index in range(owners):
        f_copy(index).wait_recv()

    square = jnp.zeros((1, 1), F32)
    tall = extent // STRIPES
    for i in range(STRIPES):
        values = gbuf[pl.ds(i * tall, tall), :].astype(F32)
        square += jnp.sum(values * values, axis=(0, 1), keepdims=True)
    mean = square / extent
    damping = DAMPING * mean + EPSILON
    rate = 0.25 / (2.0 * (mean + damping))

    def diagonal(i):
        row = lax.broadcasted_iota(jnp.int32, (tall, extent), 0) + i * tall
        column = lax.broadcasted_iota(jnp.int32, (tall, extent), 1)
        return row == column

    @pl.when(core == 0)
    def _():
        for i in range(STRIPES):
            work[pl.ds(i * tall, tall), :] = product(
                gbuf[pl.ds(i * tall, tall), :], gbuf[...], ((1,), (1,))
            )

    @pl.when(core == 1)
    def _():
        for i in range(STRIPES):
            work[pl.ds(i * tall, tall), :] = product(
                gbuf[:, pl.ds(i * tall, tall)], gbuf[...], ((0,), (0,))
            )

    for i in range(STRIPES):
        stripe = pl.ds(i * tall, tall)
        shift = jnp.where(diagonal(i), (1.25 - MEAN) - damping * rate, 0.0)
        error = shift - work[stripe, :] * rate
        work[stripe, :] = error
        high1[stripe, :], low1[stripe, :] = split(error)

    def precise(stripe, left_high, left_low, right_high, right_low):
        return (
            product(left_high[stripe, :], right_high[...])
            + product(left_high[stripe, :], right_low[...])
            + product(left_low[stripe, :], right_high[...])
        )

    for i in range(STRIPES):
        stripe = pl.ds(i * tall, tall)
        error = work[stripe, :]
        squared = precise(stripe, high1, low1, high1, low1) + (2 * MEAN) * error
        half[stripe, :] = squared
        high2[stripe, :], low2[stripe, :] = split(squared)
    for i in range(STRIPES):
        stripe = pl.ds(i * tall, tall)
        high1[stripe, :], low1[stripe, :] = split(5.0 * work[stripe, :] - 4.0 * half[stripe, :])

    mean2 = MEAN * MEAN
    mean4 = mean2 * mean2
    remain = 5.0 * MEAN - 4.0 * mean2

    def r_copy(i, buffer):
        return pltpu.make_async_remote_copy(
            src_ref=buffer.at[pl.ds(i * tall, tall)],
            dst_ref=buffer.at[pl.ds(i * tall, tall)],
            send_sem=r_send.at[i],
            recv_sem=r_recv.at[i],
            device_id=sibling,
            device_id_type=MESH,
        )

    for i in range(STRIPES):
        stripe = pl.ds(i * tall, tall)
        squared = half[stripe, :]
        fourth = precise(stripe, high2, low2, high2, low2) + (2 * mean2) * squared
        fourth_high, fourth_low = split(fourth)
        error = work[stripe, :]
        mapped = (
            product(fourth_high, high1[...])
            + product(fourth_high, low1[...])
            + product(fourth_low, high1[...])
            + mean4 * (5.0 * error - 4.0 * squared)
            + remain * fourth
        )
        root = (5.0 * error - mapped) * 0.25
        root += jnp.where(diagonal(i), (5.0 * MEAN - mean4 * remain) * 0.25, 0.0)
        rounded = root.astype(BF16)

        @pl.when(core == 0)
        def _():
            inner[stripe, :] = product(rounded, gbuf[...]).astype(BF16)
            r_copy(i, inner).start()

        @pl.when(core == 1)
        def _():
            rroot[stripe, :] = rounded
            r_copy(i, rroot).start()

    for i in range(STRIPES):
        @pl.when(core == 0)
        def _():
            r_copy(i, rroot).wait_recv()

        @pl.when(core == 1)
        def _():
            r_copy(i, inner).wait_recv()

    total = jnp.zeros((1, 1), F32)
    for i in range(STRIPES):
        stripe = pl.ds(i * tall, tall)
        raw = product(inner[stripe, :], rroot[...])
        work[stripe, :] = raw
        total += jnp.sum(raw * raw, axis=(0, 1), keepdims=True)

    spot = place // 2
    hosted = jnp.where(fullest, own_live > extra + spot, other_live > owners + spot)
    live = jnp.where(lax.rem(place, 2) == 0, own_live > spot, hosted)
    flag = jnp.where(live, 1.0, 0.0).astype(F32)
    entries = float(extent * extent)
    scale = flag * jnp.sqrt(square / entries) / jnp.sqrt(total / entries + EPSILON)

    def o_copy(target, source_place):
        return pltpu.make_async_remote_copy(
            src_ref=outgoing.at[target],
            dst_ref=ret.at[source_place],
            send_sem=o_send.at[target],
            recv_sem=o_recv.at[source_place],
            device_id={"block": target},
            device_id_type=MESH,
        )

    def y_copy(k):
        return pltpu.make_async_remote_copy(
            src_ref=ret.at[2 * k + 1],
            dst_ref=xret.at[k],
            send_sem=y_send.at[k],
            recv_sem=y_recv.at[k],
            device_id=across,
            device_id_type=MESH,
        )

    home = pltpu.make_async_copy(outgoing.at[place], ret.at[place], local_sem)
    for step in range(owners - 1, -1, -1):
        target = lax.rem(place + step, owners)
        outgoing[target] = (work[own_rows(target), :] * scale).astype(BF16)
        if step:
            o_copy(target, place).start()
        else:
            home.start()

    for owner in range(owners):
        @pl.when(place != owner)
        def _():
            o_copy(place, owner).wait_recv()

        @pl.when(place == owner)
        def _():
            home.wait()

        if owner % 2:
            y_copy(owner // 2).start()

    for i in range(3):
        pair_copy(i).wait_send()
    for k in range(extra):
        x_copy(k).wait_send()
    for owner in range(owners):
        f_copy(owner).wait_send()

        @pl.when(place != owner)
        def _():
            z_copy(owner, chosen.at[0], place).wait_send()
            o_copy(owner, place).wait_send()
    for i in range(STRIPES):
        r_copy(i, inner).wait_send()
    for k in range(extra):
        y_copy(k).wait()


def shards(grad_parts, live_counts):
    grad_shard = grad_parts[0, 0]
    owners = lax.axis_size("block")
    extra = owners // 2
    slots, rows, extent = grad_shard.shape
    part = rows // 2
    sent = owners + extra
    dma = pltpu.SemaphoreType.DMA
    wide = (extent, extent)
    ret, xret = pl.pallas_call(
        refresh,
        out_shape=(
            jax.ShapeDtypeStruct((owners, part, extent), BF16),
            jax.ShapeDtypeStruct((extra, part, extent), BF16),
        ),
        in_specs=[pl.BlockSpec(memory_space=pltpu.SMEM), pl.BlockSpec(memory_space=pl.ANY)],
        out_specs=[pl.BlockSpec(memory_space=pl.ANY)] * 2,
        scratch_shapes=[
            pltpu.VMEM((sent, part, extent), BF16),
            pltpu.VMEM((sent, part, extent), BF16),
            pltpu.VMEM((sent, part, extent), BF16),
            pltpu.VMEM((extra, part, extent), BF16),
            pltpu.VMEM((extra, part, extent), BF16),
            pltpu.VMEM(wide, BF16),
            pltpu.VMEM(wide, F32),
            pltpu.VMEM(wide, F32),
            pltpu.VMEM(wide, BF16),
            pltpu.VMEM(wide, BF16),
            pltpu.VMEM(wide, BF16),
            pltpu.VMEM(wide, BF16),
            pltpu.VMEM(wide, BF16),
            pltpu.VMEM(wide, BF16),
            pltpu.VMEM((owners, part, extent), BF16),
            dma((3,)), dma((3,)), dma((3,)),
            dma((extra,)), dma((extra,)),
            dma((owners,)), dma((owners,)),
            dma((owners,)), dma((owners,)),
            dma((STRIPES,)), dma((STRIPES,)),
            dma((owners,)), dma((owners,)),
            dma((extra,)), dma((extra,)),
            dma(()),
        ],
        compiler_params=pltpu.CompilerParams(
            collective_id=0, has_side_effects=True, vmem_limit_bytes=32 * 2**20
        ),
        name="refresh",
    )(live_counts, grad_shard)
    fullest = live_counts[lax.axis_index("scen")] > extra
    own_even = ret[0::2]
    zero = jnp.zeros((), BF16)
    own_odd = jnp.where(fullest, ret[1::2], zero)
    back = jnp.where(fullest, xret, zero)
    idle = jnp.zeros((slots - sent, part, extent), BF16)
    return jnp.concatenate([own_even, own_odd, back, idle], axis=0)[None]


def solution(mesh):
    in_specs = (P("dp", ("groups", "scen"), None, "block", None), P("groups"))
    out_specs = P(("groups", "scen"), None, ("block", "dp"), None)
    return jax.shard_map(shards, mesh=mesh, in_specs=in_specs, out_specs=out_specs, check_vma=False)
```

time: 132 us -> 40.2 us (0.30)
  waiting for transfers between devices: 52.9 us -> 0 us
  Pallas kernels: 0 us -> 36 us
  matrix products: 20.7 us -> 0 us
  blocking collectives: 19.9 us -> 0 us
  between operations: 13.4 us -> 0.69 us
  local copies, waits for them, and re-layouts: 11.1 us -> 2.47 us
  starting transfers between devices: 5.01 us -> 0 us
  loops' own time: 3.59 us -> 0 us
  other arithmetic: 4.41 us -> 0.89 us
    pallas_call x0 -> x1, Pallas kernels: none -> 36 us  [shards(): pl.pallas_call(refresh, out_shape=(jax.ShapeDtypeStruct((owners, part, ex...]
    all_to_all x1 -> x0, waiting for transfers between devices: 25 us -> none  [shards(): lax.all_to_all(outgoing, 'block', split_axis=1, concat_axis=1, tiled=True)]
    psum x1 -> x0, waiting for transfers between devices: 24.8 us -> none  [shards(): summed = lax.psum(partial_value.astype(jnp.bfloat16), 'dp')]
    dot_general x11 -> x0, matrix products: 20.7 us -> none  [the longest x2 4 us: newton_root(): jnp.dot(factor, factor, precision=HIGHEST, preferred_element_type=jnp.flo...]
    all_to_all x1 -> x0, blocking collectives: 17.5 us -> none  [shards(): lax.all_to_all(returning, 'block', split_axis=1, concat_axis=1, tiled=True)]
    all_to_all x1 -> x0, starting transfers between devices: 5 us -> none  [shards(): lax.all_to_all(outgoing, 'block', split_axis=1, concat_axis=1, tiled=True)]
    another operation x3 -> x0, loops' own time: 3.59 us -> none  [the longest x2 2.31 us: single(): return lax.cond(live_flag > 0, compute, skipped, 0)]
    squeeze x4 -> x0, local copies, waits for them, and re-layouts: 2.59 us -> none  [owner_roots(): return lax.map(single, (blocks, live_flags))]
  transfers between devices with their start and end apart: 3 -> 0, of which waited for: 3 -> 0; matrix products, arithmetic and copies ran while one was open for 1% -> 0% of each run, Pallas kernels for 0% -> 0%
where the time goes in v1:
time: 40.2 us; the launch traced here: 40.1 us
  Pallas kernels  36 us (90%)
  local copies, waits for them, and re-layouts  2.47 us (6%)
  other arithmetic  0.89 us (2%)
  between operations  0.69 us (2%)
    pallas_call x1, Pallas kernels, shards(): pl.pallas_call(refresh, out_shape=(jax.ShapeDtypeStruct((owners, part, ex...  36 us
    unnamed x4, local copies, waits for them, and re-layouts  1.87 us
    broadcast_in_dim x1, other arithmetic, shards(): return jnp.concatenate([own_even, own_odd, back, idle], axis=0)[None]  0.86 us

profile of v1, /device:TPU:0, one launch (start us, length us, event | category | flops | bytes accessed | tf_op | source)
XLA Modules:
  0.0 40.1 jit_solution(18063825941988127958)
XLA Ops:
  0.0 0.0 copy-start.1
  0.0 0.7 %copy-done.1 = s32[2]{0:T(128)S(1)} copy-done((s32[2]{0:T(128)S(1)}, s32[2]{0:T(128)}, u32[]{:S(2)}) %copy-start.1) | copy-done | bytes 32
  0.7 0.6 %dynamic_slice.3 = s32[1]{0:T(128)} dynamic-slice(s32[2]{0:T(128)S(1)} %copy-done.1, s32[]{:T(128)S(6)} %select_n.15), dynamic_slice_sizes={1} | dynamic-slice | bytes 12 | tf_op jit(solution)/shard_map/dynamic_slice | solution.py:385
  1.9 0.0 copy-start
  1.9 1.2 %copy-done = bf16[1,1,8,128,512]{4,3,2,1,0:T(8,128)(2,1)S(1)} copy-done((bf16[1,1,8,128,512]{4,3,2,1,0:T(8,128)(2,1)S(1)}, bf16[1,1,8,128,512]{4,3,2,1,0:T(8,128)(2,1)}, u32[]{:S(2)}) %copy-start) | copy-done | bytes 1048600
  3.1 36.0 %refresh.1 = (bf16[4,64,512]{2,1,0:T(8,128)(2,1)S(1)}, bf16[2,64,512]{2,1,0:T(8,128)(2,1)S(1)}) custom-call(s32[2]{0:T(128)S(1)} %copy-done.1, bf16[8,128,512]{2,1,0:T(8,128)(2,1)S(1)} %bitcast.4), custom_call_target="tpu_custom_call" | custom-call | tf_op jit(solution)/shard_map/refresh/pallas_call | solution.py:347
  39.2 0.9 %maximum_bitcast_fusion = bf16[1,8,64,512]{3,2,1,0:T(8,128)(2,1)} fusion(bf16[2,64,512]{2,1,0:T(8,128)(2,1)S(1)} %broadcast_in_dim.9, bf16[2,64,512]{2,1,0:T(8,128)(2,1)S(1)} %get-tuple-element.11, bf16[2,64,512]{2,1,0:T(8,128)(2,1)S(1)} %get-tuple-element.10, bf16[2,64,512]{2,1,0:T(8,128)(2,1)S(1)} %get-tuple-element.9), kind=kLoop, calls=%fused_computation | loop fusion | flops 786432 | bytes 1048576 | tf_op jit(solution)/shard_map/broadcast_in_dim | solution.py:391
  (2 shorter events, 0.0 us)
Async XLA Ops:
  0.0 0.7 %copy-start.1 = (s32[2]{0:T(128)S(1)}, s32[2]{0:T(128)}, u32[]{:S(2)}) copy-start(s32[2]{0:T(128)} %counts.1) | copy-start | bytes 28
  1.9 1.2 %copy-start = (bf16[1,1,8,128,512]{4,3,2,1,0:T(8,128)(2,1)S(1)}, bf16[1,1,8,128,512]{4,3,2,1,0:T(8,128)(2,1)}, u32[]{:S(2)}) copy-start(bf16[1,1,8,128,512]{4,3,2,1,0:T(8,128)(2,1)} %param.2) | copy-start | bytes 3145732

commit v2 on v1

--- a/solution.py
+++ b/solution.py
@@ -1,5 +1,3 @@
-import functools
-
 import jax
 import jax.numpy as jnp
 from jax import lax
@@ -13,7 +11,7 @@
 F32 = jnp.float32
 BF16 = jnp.bfloat16
 MEAN = 1.125
-STRIPES = 4
+STRIPES = 1
 
 
 def product(a, b, contract=((1,), (0,))):
@@ -26,11 +24,11 @@
 
 
 def refresh(
-    counts, grad, ret, xret,
+    counts, grad, ret, xret, mask,
     own, peer, summed, arrived, chosen, gbuf, work, half, high1, low1, high2, low2,
-    inner, rroot, outgoing,
+    inner, rroot, outgoing, flags,
     own_sem, pair_send, pair_recv, x_send, x_recv, z_send, z_recv, f_send, f_recv,
-    r_send, r_recv, o_send, o_recv, y_send, y_recv, local_sem,
+    r_send, r_recv, o_send, o_recv, y_send, y_recv, local_sem, mask_sem,
 ):
     owners = lax.axis_size("block")
     extra = owners // 2
@@ -146,6 +144,9 @@
     own_live = counts[tower]
     other_live = counts[other_tower]
     fullest = own_live > extra
+    flags[...] = jnp.where(jnp.broadcast_to(own_live, (1, extent)) > extra, 1.0, 0.0)
+    mask_copy = pltpu.make_async_copy(flags, mask, mask_sem)
+    mask_copy.start()
     is_fullest = jnp.broadcast_to(own_live, (part, extent)) > extra
     for k in range(extra):
         x_copy(k).wait_recv()
@@ -298,7 +299,7 @@
         )
 
     home = pltpu.make_async_copy(outgoing.at[place], ret.at[place], local_sem)
-    for step in range(owners - 1, -1, -1):
+    for step in range(owners):
         target = lax.rem(place + step, owners)
         outgoing[target] = (work[own_rows(target), :] * scale).astype(BF16)
         if step:
@@ -318,6 +319,7 @@
         if owner % 2:
             y_copy(owner // 2).start()
 
+    mask_copy.wait()
     for i in range(3):
         pair_copy(i).wait_send()
     for k in range(extra):
@@ -344,14 +346,15 @@
     sent = owners + extra
     dma = pltpu.SemaphoreType.DMA
     wide = (extent, extent)
-    ret, xret = pl.pallas_call(
+    ret, xret, mask = pl.pallas_call(
         refresh,
         out_shape=(
             jax.ShapeDtypeStruct((owners, part, extent), BF16),
             jax.ShapeDtypeStruct((extra, part, extent), BF16),
+            jax.ShapeDtypeStruct((1, extent), F32),
         ),
         in_specs=[pl.BlockSpec(memory_space=pltpu.SMEM), pl.BlockSpec(memory_space=pl.ANY)],
-        out_specs=[pl.BlockSpec(memory_space=pl.ANY)] * 2,
+        out_specs=[pl.BlockSpec(memory_space=pl.ANY)] * 3,
         scratch_shapes=[
             pltpu.VMEM((sent, part, extent), BF16),
             pltpu.VMEM((sent, part, extent), BF16),
@@ -368,6 +371,7 @@
             pltpu.VMEM(wide, BF16),
             pltpu.VMEM(wide, BF16),
             pltpu.VMEM((owners, part, extent), BF16),
+            pltpu.VMEM((1, extent), F32),
             dma((3,)), dma((3,)), dma((3,)),
             dma((extra,)), dma((extra,)),
             dma((owners,)), dma((owners,)),
@@ -375,14 +379,14 @@
             dma((STRIPES,)), dma((STRIPES,)),
             dma((owners,)), dma((owners,)),
             dma((extra,)), dma((extra,)),
-            dma(()),
+            dma(()), dma(()),
         ],
         compiler_params=pltpu.CompilerParams(
             collective_id=0, has_side_effects=True, vmem_limit_bytes=32 * 2**20
         ),
         name="refresh",
     )(live_counts, grad_shard)
-    fullest = live_counts[lax.axis_index("scen")] > extra
+    fullest = mask[None] > 0.5
     own_even = ret[0::2]
     zero = jnp.zeros((), BF16)
     own_odd = jnp.where(fullest, ret[1::2], zero)

time: 40.2 us -> 35.8 us (0.89)
  Pallas kernels: 36 us -> 32.8 us
  between operations: 0.69 us -> 0.02 us
  local copies, waits for them, and re-layouts: 2.47 us -> 1.89 us
    pallas_call x1, Pallas kernels: 36 us -> 32.8 us  [shards(): pl.pallas_call(refresh, out_shape=(jax.ShapeDtypeStruct((owners, part, ex...]
    dynamic_slice x1 -> x0, local copies, waits for them, and re-layouts: 0.58 us -> none  [shards(): fullest = live_counts[lax.axis_index('scen')] > extra]
where the time goes in v2:
time: 35.8 us; the launch traced here: 35.6 us
  Pallas kernels  32.8 us (92%)
  local copies, waits for them, and re-layouts  1.89 us (5%)
  other arithmetic  0.92 us (3%)
    pallas_call x1, Pallas kernels, shards(): pl.pallas_call(refresh, out_shape=(jax.ShapeDtypeStruct((owners, part, ex...  32.8 us
    unnamed x4, local copies, waits for them, and re-layouts  1.88 us
    broadcast_in_dim x1, other arithmetic, shards(): return jnp.concatenate([own_even, own_odd, back, idle], axis=0)[None]  0.86 us

profile of v2, /device:TPU:0, one launch (start us, length us, event | category | flops | bytes accessed | tf_op | source)
XLA Modules:
  0.0 35.6 jit_solution(5350985059831257747)
XLA Ops:
  0.0 0.0 copy-start.1
  0.0 0.7 %copy-done.1 = s32[2]{0:T(128)S(1)} copy-done((s32[2]{0:T(128)S(1)}, s32[2]{0:T(128)}, u32[]{:S(2)}) %copy-start.1) | copy-done | bytes 32
  0.7 0.0 copy-start
  0.7 1.2 %copy-done = bf16[1,1,8,128,512]{4,3,2,1,0:T(8,128)(2,1)S(1)} copy-done((bf16[1,1,8,128,512]{4,3,2,1,0:T(8,128)(2,1)S(1)}, bf16[1,1,8,128,512]{4,3,2,1,0:T(8,128)(2,1)}, u32[]{:S(2)}) %copy-start) | copy-done | bytes 1048600
  1.9 32.8 %refresh.1 = (bf16[4,64,512]{2,1,0:T(8,128)(2,1)S(1)}, bf16[2,64,512]{2,1,0:T(8,128)(2,1)S(1)}, f32[1,512]{1,0:T(1,128)S(1)}) custom-call(s32[2]{0:T(128)S(1)} %copy-done.1, bf16[8,128,512]{2,1,0:T(8,128)(2,1)S(1)} %bitcast.3), custom_call_target="tpu_custom_call" | custom-call | tf_op jit(solution)/shard_map/refresh/pallas_call | solution.py:349
  34.8 0.9 %maximum_bitcast_fusion = bf16[1,8,64,512]{3,2,1,0:T(8,128)(2,1)} fusion(bf16[2,64,512]{2,1,0:T(8,128)(2,1)S(1)} %broadcast_in_dim.22, bf16[2,64,512]{2,1,0:T(8,128)(2,1)S(1)} %get-tuple-element.13, bf16[2,64,512]{2,1,0:T(8,128)(2,1)S(1)} %get-tuple-element.12, bf16[2,64,512]{2,1,0:T(8,128)(2,1)S(1)} %get-tuple-element.11), kind=kLoop, calls=%fused_computation | loop fusion | flops 786432 | bytes 1048576 | tf_op jit(solution)/shard_map/broadcast_in_dim | solution.py:395
  (3 shorter events, 0.1 us)
Async XLA Ops:
  0.0 0.7 %copy-start.1 = (s32[2]{0:T(128)S(1)}, s32[2]{0:T(128)}, u32[]{:S(2)}) copy-start(s32[2]{0:T(128)} %counts.1) | copy-start | bytes 28
  0.7 1.2 %copy-start = (bf16[1,1,8,128,512]{4,3,2,1,0:T(8,128)(2,1)S(1)}, bf16[1,1,8,128,512]{4,3,2,1,0:T(8,128)(2,1)}, u32[]{:S(2)}) copy-start(bf16[1,1,8,128,512]{4,3,2,1,0:T(8,128)(2,1)} %param.2) | copy-start | bytes 3145732

commit v3 on v2

--- a/solution.py
+++ b/solution.py
@@ -382,7 +382,7 @@
             dma(()), dma(()),
         ],
         compiler_params=pltpu.CompilerParams(
-            collective_id=0, has_side_effects=True, vmem_limit_bytes=32 * 2**20
+            collective_id=0, has_side_effects=True, vmem_limit_bytes=53 * 2**20
         ),
         name="refresh",
     )(live_counts, grad_shard)

time: 35.8 us -> 34.5 us (0.964)
  local copies, waits for them, and re-layouts: 1.89 us -> 0.67 us
    unnamed x4 -> x2, local copies, waits for them, and re-layouts: 1.88 us -> 0.65 us
where the time goes in v3:
time: 34.5 us; the launch traced here: 34.4 us
  Pallas kernels  32.8 us (95%)
  other arithmetic  0.92 us (3%)
  local copies, waits for them, and re-layouts  0.67 us (2%)
    pallas_call x1, Pallas kernels, shards(): pl.pallas_call(refresh, out_shape=(jax.ShapeDtypeStruct((owners, part, ex...  32.8 us
    broadcast_in_dim x1, other arithmetic, shards(): return jnp.concatenate([own_even, own_odd, back, idle], axis=0)[None]  0.86 us

profile of v3, /device:TPU:0, one launch (start us, length us, event | category | flops | bytes accessed | tf_op | source)
XLA Modules:
  0.0 34.4 jit_solution(9088651125592444801)
XLA Ops:
  0.0 0.0 copy-start
  0.0 0.7 %copy-done = s32[2]{0:T(128)S(1)} copy-done((s32[2]{0:T(128)S(1)}, s32[2]{0:T(128)}, u32[]{:S(2)}) %copy-start) | copy-done | bytes 32
  0.7 32.8 %refresh.1 = (bf16[4,64,512]{2,1,0:T(8,128)(2,1)S(1)}, bf16[2,64,512]{2,1,0:T(8,128)(2,1)S(1)}, f32[1,512]{1,0:T(1,128)S(1)}) custom-call(s32[2]{0:T(128)S(1)} %copy-done, bf16[8,128,512]{2,1,0:T(8,128)(2,1)} %bitcast.3), custom_call_target="tpu_custom_call" | custom-call | tf_op jit(solution)/shard_map/refresh/pallas_call | solution.py:349
  33.5 0.9 %maximum_bitcast_fusion = bf16[1,8,64,512]{3,2,1,0:T(8,128)(2,1)} fusion(bf16[2,64,512]{2,1,0:T(8,128)(2,1)S(1)} %broadcast_in_dim.22, bf16[2,64,512]{2,1,0:T(8,128)(2,1)S(1)} %get-tuple-element.13, bf16[2,64,512]{2,1,0:T(8,128)(2,1)S(1)} %get-tuple-element.12, bf16[2,64,512]{2,1,0:T(8,128)(2,1)S(1)} %get-tuple-element.11), kind=kLoop, calls=%fused_computation | loop fusion | flops 786432 | bytes 1048576 | tf_op jit(solution)/shard_map/broadcast_in_dim | solution.py:395
  (3 shorter events, 0.1 us)
Async XLA Ops:
  0.0 0.7 %copy-start = (s32[2]{0:T(128)S(1)}, s32[2]{0:T(128)}, u32[]{:S(2)}) copy-start(s32[2]{0:T(128)} %counts.1) | copy-start | bytes 28

commit v4 on v3

--- a/solution.py
+++ b/solution.py
@@ -197,22 +197,17 @@
         work[stripe, :] = error
         high1[stripe, :], low1[stripe, :] = split(error)
 
-    def precise(stripe, left_high, left_low, right_high, right_low):
-        return (
-            product(left_high[stripe, :], right_high[...])
-            + product(left_high[stripe, :], right_low[...])
-            + product(left_low[stripe, :], right_high[...])
-        )
+    def precise(stripe, high, low):
+        cross = product(high[...], low[...])
+        return product(high[...], high[...]) + (cross + cross.T)
 
     for i in range(STRIPES):
         stripe = pl.ds(i * tall, tall)
         error = work[stripe, :]
-        squared = precise(stripe, high1, low1, high1, low1) + (2 * MEAN) * error
+        squared = precise(stripe, high1, low1) + (2 * MEAN) * error
         half[stripe, :] = squared
         high2[stripe, :], low2[stripe, :] = split(squared)
-    for i in range(STRIPES):
-        stripe = pl.ds(i * tall, tall)
-        high1[stripe, :], low1[stripe, :] = split(5.0 * work[stripe, :] - 4.0 * half[stripe, :])
+        high1[stripe, :], low1[stripe, :] = split(5.0 * error - 4.0 * squared)
 
     mean2 = MEAN * MEAN
     mean4 = mean2 * mean2
@@ -231,7 +226,7 @@
     for i in range(STRIPES):
         stripe = pl.ds(i * tall, tall)
         squared = half[stripe, :]
-        fourth = precise(stripe, high2, low2, high2, low2) + (2 * mean2) * squared
+        fourth = precise(stripe, high2, low2) + (2 * mean2) * squared
         fourth_high, fourth_low = split(fourth)
         error = work[stripe, :]
         mapped = (

time: 34.5 us -> 34 us (0.986)
  Pallas kernels: 32.8 us -> 32.3 us
    pallas_call x1, Pallas kernels: 32.8 us -> 32.3 us  [shards(): pl.pallas_call(refresh, out_shape=(jax.ShapeDtypeStruct((owners, part, ex...]
where the time goes in v4:
time: 34 us; the launch traced here: 33.9 us
  Pallas kernels  32.3 us (95%)
  other arithmetic  0.92 us (3%)
  local copies, waits for them, and re-layouts  0.67 us (2%)
    pallas_call x1, Pallas kernels, shards(): pl.pallas_call(refresh, out_shape=(jax.ShapeDtypeStruct((owners, part, ex...  32.3 us
    broadcast_in_dim x1, other arithmetic, shards(): return jnp.concatenate([own_even, own_odd, back, idle], axis=0)[None]  0.86 us

profile of v4, /device:TPU:0, one launch (start us, length us, event | category | flops | bytes accessed | tf_op | source)
XLA Modules:
  0.0 33.9 jit_solution(4494676367659033552)
XLA Ops:
  0.0 0.0 copy-start
  0.0 0.7 %copy-done = s32[2]{0:T(128)S(1)} copy-done((s32[2]{0:T(128)S(1)}, s32[2]{0:T(128)}, u32[]{:S(2)}) %copy-start) | copy-done | bytes 32
  0.7 32.3 %refresh.1 = (bf16[4,64,512]{2,1,0:T(8,128)(2,1)S(1)}, bf16[2,64,512]{2,1,0:T(8,128)(2,1)S(1)}, f32[1,512]{1,0:T(1,128)S(1)}) custom-call(s32[2]{0:T(128)S(1)} %copy-done, bf16[8,128,512]{2,1,0:T(8,128)(2,1)} %bitcast.3), custom_call_target="tpu_custom_call" | custom-call | tf_op jit(solution)/shard_map/refresh/pallas_call | solution.py:344
  33.0 0.9 %maximum_bitcast_fusion = bf16[1,8,64,512]{3,2,1,0:T(8,128)(2,1)} fusion(bf16[2,64,512]{2,1,0:T(8,128)(2,1)S(1)} %broadcast_in_dim.22, bf16[2,64,512]{2,1,0:T(8,128)(2,1)S(1)} %get-tuple-element.13, bf16[2,64,512]{2,1,0:T(8,128)(2,1)S(1)} %get-tuple-element.12, bf16[2,64,512]{2,1,0:T(8,128)(2,1)S(1)} %get-tuple-element.11), kind=kLoop, calls=%fused_computation | loop fusion | flops 786432 | bytes 1048576 | tf_op jit(solution)/shard_map/broadcast_in_dim | solution.py:390
  (3 shorter events, 0.1 us)
Async XLA Ops:
  0.0 0.7 %copy-start = (s32[2]{0:T(128)S(1)}, s32[2]{0:T(128)}, u32[]{:S(2)}) copy-start(s32[2]{0:T(128)} %counts.1) | copy-start | bytes 28

commit v5 on v4

--- a/solution.py
+++ b/solution.py
@@ -159,14 +159,17 @@
         source = lax.rem(place + step, owners)
         z_copy(place, chosen.at[0], source).wait_recv()
         f_copy(source).start()
+    square = jnp.zeros((1, extent), F32)
+    for index in range(owners):
+        values = gbuf[own_rows(index), :].astype(F32)
+        square += jnp.sum(values * values, axis=0, keepdims=True)
     for index in range(owners):
         f_copy(index).wait_recv()
-
-    square = jnp.zeros((1, 1), F32)
+        values = gbuf[pl.ds(aligned(index * rows + (1 - core) * part), part), :].astype(F32)
+        square += jnp.sum(values * values, axis=0, keepdims=True)
+    square = jnp.sum(square, axis=1, keepdims=True)
+
     tall = extent // STRIPES
-    for i in range(STRIPES):
-        values = gbuf[pl.ds(i * tall, tall), :].astype(F32)
-        square += jnp.sum(values * values, axis=(0, 1), keepdims=True)
     mean = square / extent
     damping = DAMPING * mean + EPSILON
     rate = 0.25 / (2.0 * (mean + damping))
@@ -283,9 +286,9 @@
             device_id_type=MESH,
         )
 
-    def y_copy(k):
-        return pltpu.make_async_remote_copy(
-            src_ref=ret.at[2 * k + 1],
+    def y_copy(k, source):
+        return pltpu.make_async_remote_copy(
+            src_ref=source,
             dst_ref=xret.at[k],
             send_sem=y_send.at[k],
             recv_sem=y_recv.at[k],
@@ -302,18 +305,22 @@
         else:
             home.start()
 
-    for owner in range(owners):
-        @pl.when(place != owner)
-        def _():
-            o_copy(place, owner).wait_recv()
-
-        @pl.when(place == owner)
-        def _():
-            home.wait()
-
-        if owner % 2:
-            y_copy(owner // 2).start()
-
+            @pl.when(lax.rem(place, 2) == 1)
+            def _():
+                y_copy(place // 2, outgoing.at[place]).start()
+
+    for k in range(extra):
+        @pl.when(place != 2 * k + 1)
+        def _():
+            o_copy(place, 2 * k + 1).wait_recv()
+            y_copy(k, ret.at[2 * k + 1]).start()
+
+    for k in range(extra):
+        @pl.when(place != 2 * k)
+        def _():
+            o_copy(place, 2 * k).wait_recv()
+
+    home.wait()
     mask_copy.wait()
     for i in range(3):
         pair_copy(i).wait_send()
@@ -329,7 +336,7 @@
     for i in range(STRIPES):
         r_copy(i, inner).wait_send()
     for k in range(extra):
-        y_copy(k).wait()
+        y_copy(k, ret.at[2 * k + 1]).wait()
 
 
 def shards(grad_parts, live_counts):

time: 34 us -> 33.8 us (level)
  no operation moved by 1% of the time
where the time goes in v5:
time: 33.8 us; the launch traced here: 33.6 us
  Pallas kernels  32 us (95%)
  other arithmetic  0.92 us (3%)
  local copies, waits for them, and re-layouts  0.67 us (2%)
    pallas_call x1, Pallas kernels, shards(): pl.pallas_call(refresh, out_shape=(jax.ShapeDtypeStruct((owners, part, ex...  32 us
    broadcast_in_dim x1, other arithmetic, shards(): return jnp.concatenate([own_even, own_odd, back, idle], axis=0)[None]  0.86 us

profile of v5, /device:TPU:0, one launch (start us, length us, event | category | flops | bytes accessed | tf_op | source)
XLA Modules:
  0.0 33.6 jit_solution(7143474828543649769)
XLA Ops:
  0.0 0.0 copy-start
  0.0 0.7 %copy-done = s32[2]{0:T(128)S(1)} copy-done((s32[2]{0:T(128)S(1)}, s32[2]{0:T(128)}, u32[]{:S(2)}) %copy-start) | copy-done | bytes 32
  0.7 32.0 %refresh.1 = (bf16[4,64,512]{2,1,0:T(8,128)(2,1)S(1)}, bf16[2,64,512]{2,1,0:T(8,128)(2,1)S(1)}, f32[1,512]{1,0:T(1,128)S(1)}) custom-call(s32[2]{0:T(128)S(1)} %copy-done, bf16[8,128,512]{2,1,0:T(8,128)(2,1)} %bitcast.3), custom_call_target="tpu_custom_call" | custom-call | tf_op jit(solution)/shard_map/refresh/pallas_call | solution.py:351
  32.8 0.9 %maximum_bitcast_fusion = bf16[1,8,64,512]{3,2,1,0:T(8,128)(2,1)} fusion(bf16[2,64,512]{2,1,0:T(8,128)(2,1)S(1)} %broadcast_in_dim.22, bf16[2,64,512]{2,1,0:T(8,128)(2,1)S(1)} %get-tuple-element.13, bf16[2,64,512]{2,1,0:T(8,128)(2,1)S(1)} %get-tuple-element.12, bf16[2,64,512]{2,1,0:T(8,128)(2,1)S(1)} %get-tuple-element.11), kind=kLoop, calls=%fused_computation | loop fusion | flops 786432 | bytes 1048576 | tf_op jit(solution)/shard_map/broadcast_in_dim | solution.py:397
  (3 shorter events, 0.1 us)
Async XLA Ops:
  0.0 0.7 %copy-start = (s32[2]{0:T(128)S(1)}, s32[2]{0:T(128)}, u32[]{:S(2)}) copy-start(s32[2]{0:T(128)} %counts.1) | copy-start | bytes 28
